TPU v7x, 32 devices: a whole 2x2x4 slice. The times are simulated.
32 devices in a mesh: dp: 4 (over y, core), tensor: 8 (over z, x).
Axes of the slice: x: 2, y: 2, z: 4, core: 2. Of those that a mesh axis runs over, the one named last changes fastest.
Arguments:
- tokens: bfloat16 [16384, 3072], P(('dp', 'tensor')), parts along dimension 0, may hold values from -6 to 6
- expert_ids: int32 [16384, 4], P(('dp', 'tensor')), parts along dimension 0, may hold values from 0 to 15, as said below
- gate_probs: float32 [16384, 4], P(('dp', 'tensor')), parts along dimension 0, may hold values from 0.1 to 1
- gate_weight: bfloat16 [3072, 5376], P(None, 'tensor'), may hold values from -0.109375 to 0.109375
- up_weight: bfloat16 [3072, 5376], P(None, 'tensor'), may hold values from -0.109375 to 0.109375
- down_weight: bfloat16 [5376, 3072], P('tensor'), may hold values from -0.078125 to 0.078125
Outputs:
- mixed: bfloat16 [16384, 3072], P(('dp', 'tensor')), parts along dimension 0
There are 4 independent parts, one for each index of `dp`. A program takes and returns all parts, laid end to end along the dimension named above; an argument that names none is the same for every part. Nothing has to cross between parts.
Inputs may be any that keep to these rules, and one draw needn't show every extreme that they name: `expert_ids`: each row names 4 different experts. In each block of 128 consecutive tokens (rows b * 128 to (b + 1) * 128 - 1) between 1 and 32 rows name expert 0, and some block has exactly 32.
All inputs are finite; a program needn't handle non-finite values.
Results may differ from a plain program's by a relative error of at most 0.019.
Values may be sent and summed in bfloat16 or wider, within the bound.
A program may use at most 128 MiB of HBM per device.

v0:
```python
import jax
import jax.numpy as jnp
from jax import lax
from jax.sharding import PartitionSpec as P

SPANS = 4
CT = 128
CAP = 32


def on_device(tokens, expert_ids, gate_probs, gate_weight, up_weight, down_weight):
    model_width = tokens.shape[1]
    is_window = expert_ids == 0
    routed = jnp.any(is_window, axis=1)
    gate_share = jnp.sum(jnp.where(is_window, gate_probs, 0.0), axis=1)
    routed_blocks = routed.reshape(SPANS, CT)
    slot_place = jnp.cumsum(routed_blocks.astype(jnp.int32), axis=1) - 1
    selector = (
        slot_place[:, None, :] == jnp.arange(CAP, dtype=jnp.int32)[None, :, None]
    ) & routed_blocks[:, None, :]
    slot_rows = jnp.einsum(
        "bst,btd->bsd",
        selector.astype(jnp.bfloat16),
        tokens.reshape(SPANS, CT, model_width),
        preferred_element_type=jnp.float32,
    ).astype(jnp.bfloat16)
    row_piece = lax.all_gather(
        slot_rows.reshape(SPANS * CAP, model_width), "tensor", axis=0, tiled=True
    )
    gate_pre = jnp.dot(row_piece, gate_weight, preferred_element_type=jnp.float32)
    up_pre = jnp.dot(row_piece, up_weight, preferred_element_type=jnp.float32)
    hidden = (jax.nn.silu(gate_pre) * up_pre).astype(jnp.bfloat16)
    partial_rows = jnp.dot(hidden, down_weight, preferred_element_type=jnp.float32)
    expert_out = lax.psum_scatter(
        partial_rows.astype(jnp.bfloat16), "tensor", scatter_dimension=0, tiled=True
    ).astype(jnp.float32)
    slot_index = jnp.where(
        routed_blocks, jnp.arange(SPANS, dtype=jnp.int32)[:, None] * CAP + slot_place, 0
    )
    picked = jnp.take(expert_out, slot_index.reshape(-1), axis=0)
    mixed = jnp.where(routed[:, None], gate_share[:, None] * picked, 0.0)
    return mixed.astype(jnp.bfloat16)


def solution(mesh):
    in_specs = (
        P(("dp", "tensor"), None),
        P(("dp", "tensor"), None),
        P(("dp", "tensor"), None),
        P(None, "tensor"),
        P(None, "tensor"),
        P("tensor", None),
    )
    out_specs = P(("dp", "tensor"), None)
    return jax.shard_map(
        on_device, mesh=mesh, in_specs=in_specs, out_specs=out_specs, check_vma=False
    )
```

profile of v0, /device:TPU:0, one launch (start us, length us, event | category | flops | bytes accessed | tf_op | source)
XLA Modules:
  0.0 277.2 jit_solution(13292705280469679699)
XLA Ops:
  6.5 0.0 copy-start
  6.5 0.0 all-gather.2.cloned.1.call-start
  6.5 0.9 select_reduce_fusion
  7.5 0.3 reduce_window_sum.11
  7.8 0.7 copy-done
  8.5 1.4 convolution_convert_fusion.1
  9.9 0.0 all-gather.2.cloned.1.call-update
  9.9 0.0 reduce-scatter.2.cloned.1.call-start
  9.9 101.8 %all-gather.2.cloned.1.call-done = bf16[1024,3072]{1,0:T(8,128)(2,1)} async-done(((bf16[128,3072]{1,0:T(8,128)(2,1)}), bf16[1024,3072]{1,0:T(8,128)(2,1)}) %all-gather.2.cloned.1.call-update) | async-done | bytes 6291472 | tf_op jit(solution)/shard_map/all_gather | solution.py:27
  111.8 10.0 %fusion.4 = f32[1024,672]{0,1:T(8,128)} fusion(bf16[1024,3072]{1,0:T(8,128)(2,1)} %all-gather.2.cloned.1.call-done, bf16[3072,672]{0,1:T(8,128)(2,1)} %param.9), kind=kOutput, calls=%fused_computation.21 | convolution fusion | flops 4227858432 | bytes 13172736 | tf_op jit(solution)/shard_map/dot_general | solution.py:30
  121.7 16.3 %convolution_convert_fusion = bf16[1024,3072]{1,0:T(8,128)(2,1)} fusion(bf16[672,3072]{1,0:T(8,128)(2,1)} %param.11, f32[1024,672]{0,1:T(8,128)} %fusion.4, bf16[1024,3072]{1,0:T(8,128)(2,1)} %all-gather.2.cloned.1.call-done, bf16[3072,672]{0,1:T(8,128)(2,1)} %param.10), kind=kOutput, calls=%fused_computation.2 | convolution fusion | flops 8462991360 | bytes 23592960 | tf_op jit(solution)/shard_map/dot_general | solution.py:33
  138.1 0.0 reduce-scatter.2.cloned.1.call-update
  138.1 0.1 compare_and_fusion
  138.2 116.2 %reduce-scatter.2.cloned.1.call-done = bf16[128,3072]{1,0:T(8,128)(2,1)} async-done(((bf16[1024,3072]{1,0:T(8,128)(2,1)}), bf16[128,3072]{1,0:T(8,128)(2,1)}) %reduce-scatter.2.cloned.1.call-update) | async-done | bytes 786448 | tf_op jit(solution)/shard_map/reduce_scatter | solution.py:34
  254.4 2.4 convert_element_type.23
  256.8 8.7 %gather_fusion = f32[512,3072]{1,0:T(8,128)} fusion(f32[128,3072]{1,0:T(8,128)} %convert_element_type.23, s32[1024]{0:T(1024)S(1)} %pad_clamp_fusion), kind=kCustom, calls=%fused_computation | custom fusion | bytes 12584960 | tf_op jit(solution)/shard_map/jit(_take)/gather | solution.py:40
  265.5 4.9 %select_convert_fusion = bf16[512,3072]{1,0:T(8,128)(2,1)} fusion(f32[512,3072]{1,0:T(8,128)} %gather_fusion, f32[512]{0:T(512)S(1)} %get-tuple-element.7, pred[512]{0:T(512)(128)(4,1)S(1)} %get-tuple-element.5, pred[512]{0:T(512)(128)(4,1)S(1)} %reduce_or.11), kind=kLoop, calls=%fused_computation.1 | loop fusion | flops 6291456 | bytes 9440256 | tf_op jit(solution)/shard_map/convert_element_type | solution.py:42
  (6 shorter events, 0.1 us)
Async XLA Ops:
  6.5 1.9 copy-start
  6.5 105.2 %all-gather.2.cloned.1.call-start = ((), (), s32[]{:S(2)}) async-start(), calls=%async_computation.1 | async-start | bytes 7077888 | tf_op jit(solution)/shard_map/all_gather | solution.py:27
  9.9 244.5 %reduce-scatter.2.cloned.1.call-start = ((), (), s32[]{:S(2)}) async-start(), calls=%async_computation.2 | async-start | bytes 7077888 | tf_op jit(solution)/shard_map/reduce_scatter | solution.py:34
Sparse Core Ops, SparseCore 0:
  10.0 101.7 all-gather.1
  138.2 116.1 reduce-scatter.1
where the time goes:
time: 277 us
  waiting for transfers between devices  218 us (79%)
  matrix products  27.7 us (10%)
  between operations  13.4 us (5%)
  local copies, waits for them, and re-layouts  9.41 us (3%)
  other arithmetic  8.61 us (3%)
    reduce_scatter x1, waiting for transfers between devices, on_device(): lax.psum_scatter(partial_rows.astype(jnp.bfloat16), 'tensor', scatter_dim...  116 us
    all_gather x1, waiting for transfers between devices, on_device(): lax.all_gather(slot_rows.reshape(SPANS * CAP, model_width), 'tensor', axi...  102 us
    dot_general x1, matrix products, on_device(): jnp.dot(hidden, down_weight, preferred_element_type=jnp.float32)  16.3 us
    dot_general x1, matrix products, on_device(): jnp.dot(row_piece, gate_weight, preferred_element_type=jnp.float32)  9.97 us
    gather x1, local copies, waits for them, and re-layouts, on_device(): picked = jnp.take(expert_out, slot_index.reshape(-1), axis=0)  8.72 us
  transfers between devices with their start and end apart: 2, of which 2 were waited for; matrix products, arithmetic and copies ran while one was open for 0% of the time, Pallas kernels for 0%

commit v1 on v0

v1 whole, which is shorter than its diff:
```python
import functools

import jax
import jax.numpy as jnp
from jax import lax
from jax.experimental import pallas as pl
from jax.experimental.pallas import tpu as pltpu
from jax.sharding import PartitionSpec as P

CT = 128
CAP = 32
ROWS_Z = 4
MESH = pl.DeviceIdType.MESH


def expert_kernel(
    zs, xs, ra, wide,
    slot_ref, gw_hbm, uw_hbm, dw_hbm, out_ref,
    g, p, rz, rxa, rxb, h, gw, uw, dw,
    wsem, agz_s, agz_r, axa_s, axa_r, axb_s, axb_r,
    rz_s, rz_r, rxa_s, rxa_r, rxb_s, rxb_r,
):
    rows, width = slot_ref.shape
    rb = rows - ra
    hidden = gw.shape[1]
    me = lax.axis_index("tensor")
    dp = lax.axis_index("dp")
    z = me // xs
    x = me % xs

    def dev(zz, xx):
        return (dp, zz * xs + xx)

    def a_rows(sx):
        return pl.ds(pl.multiple_of(sx * rows, 16), ra)

    def b_rows(sx):
        return pl.ds(pl.multiple_of(sx * rows + ra, 16), rb)

    def other(k):
        return (x + k) % xs

    def source(k):
        return (x + xs - k) % xs

    def unit_rows(unit):
        return a_rows(x) if unit is None else b_rows(unit)

    def unit_sem(unit):
        return 0 if unit is None else 1 + unit

    def slot_rows(unit):
        if unit is None:
            return pl.ds(0, ra)
        return pl.ds(pl.multiple_of(ra + unit * rb, 16), rb)

    units = [None] + list(range(xs))

    def copy(src, dst, s, r, to):
        return pltpu.make_async_remote_copy(
            src_ref=src, dst_ref=dst, send_sem=s, recv_sem=r,
            device_id=to, device_id_type=MESH,
        )

    def gather_z(d, s, unit):
        part = g.at[s, unit_rows(unit)]
        i = unit_sem(unit)
        return copy(part, part, agz_s.at[d, s, i], agz_r.at[s, i], dev(z + 2 * d - 1, x))

    def gather_xa(k, s, sx):
        part = g.at[s, a_rows(sx)]
        return copy(part, part, axa_s.at[s, k - 1], axa_r.at[s, k - 1], dev(z, other(k)))

    def gather_xb(k, sx):
        part = g.at[z, b_rows(sx)]
        return copy(part, part, axb_s.at[k - 1], axb_r.at[k - 1], dev(z, other(k)))

    def reduce_xa(k, s):
        return copy(
            p.at[s, a_rows(other(k))], rxa.at[k - 1, s],
            rxa_s.at[s, k - 1], rxa_r.at[s, k - 1], dev(z, other(k)),
        )

    def reduce_xb(k):
        return copy(
            p.at[z, b_rows(other(k))], rxb.at[k - 1],
            rxb_s.at[k - 1], rxb_r.at[k - 1], dev(z, other(k)),
        )

    def reduce_z(d, o, unit):
        i = unit_sem(unit)
        return copy(
            p.at[o, unit_rows(unit)], rz.at[d, o, slot_rows(unit)],
            rz_s.at[d, o, i], rz_r.at[d, o, i], dev(z + 2 * d - 1, x),
        )

    def has_next(d):
        return z < zs - 1 if d == 1 else z > 0

    weights = [
        pltpu.make_async_copy(a, b, wsem.at[i])
        for i, (a, b) in enumerate(((gw_hbm, gw), (uw_hbm, uw), (dw_hbm, dw)))
    ]
    for w in weights:
        w.start()

    barrier = pltpu.get_barrier_semaphore()
    for d in (0, 1):
        @pl.when(has_next(d))
        def _():
            pl.semaphore_signal(barrier, inc=1, device_id=dev(z + 2 * d - 1, x), device_id_type=MESH)
    for k in range(1, xs):
        pl.semaphore_signal(barrier, inc=1, device_id=dev(z, other(k)), device_id_type=MESH)
    g[z, pl.ds(pl.multiple_of(x * rows, 16), rows), :] = slot_ref[...]
    ends = (z == 0).astype(jnp.int32) + (z == zs - 1).astype(jnp.int32)
    pl.semaphore_wait(barrier, xs + 1 - ends)

    for k in range(1, xs):
        gather_xb(k, x).start()
    for d in (0, 1):
        @pl.when(has_next(d))
        def _():
            gather_z(d, z, None).start()
            gather_z(d, z, x).start()
    for k in range(1, xs):
        gather_xa(k, z, x).start()

    @pl.when(z == zs - 1)
    def _():
        rz[0] = jnp.zeros(rz.shape[1:], rz.dtype)

    @pl.when(z == 0)
    def _():
        rz[1] = jnp.zeros(rz.shape[1:], rz.dtype)

    for k in range(1, xs):
        gather_xb(k, source(k)).wait_recv()
        for d in (0, 1):
            @pl.when(has_next(d))
            def _():
                gather_z(d, z, source(k)).start()

    def compute(s):
        for k in range(1, xs):
            gather_xa(k, s, source(k)).wait_recv()
        for c in range(0, hidden, 256):
            n = min(256, hidden - c)
            lhs = g[s]
            gate = jnp.dot(lhs, gw[:, c:c + n], preferred_element_type=jnp.float32)
            up = jnp.dot(lhs, uw[:, c:c + n], preferred_element_type=jnp.float32)
            h[:, c:c + n] = (gate / (1.0 + jnp.exp(-gate)) * up).astype(h.dtype)

        def columns(i, carry):
            at = pl.ds(pl.multiple_of(i * wide, 128), wide)
            p[s, :, at] = jnp.dot(
                h[...], dw[:, at], preferred_element_type=jnp.float32
            ).astype(p.dtype)
            return carry

        lax.fori_loop(0, width // wide, columns, 0)
        for k in range(1, xs):
            reduce_xa(k, s).start()

    for w in weights:
        w.wait()
    compute(z)

    def add_rows(count, target, parts):
        def body(i, carry):
            i = pl.multiple_of(i * 16, 16)
            total = None
            for part in parts:
                value = part(pl.ds(i, 16)).astype(jnp.float32)
                total = value if total is None else total + value
            target(i, total)
            return carry

        lax.fori_loop(0, count // 16, body, 0)

    def p_part(o, unit):
        base = x * rows if unit is None else unit * rows + ra

        def read(at):
            return p[o, pl.ds(pl.multiple_of(base + at.start, 16), 16), :]

        def write(i, value):
            p[o, pl.ds(pl.multiple_of(base + i, 16), 16), :] = value.astype(p.dtype)

        return read, write

    def rz_part(d, o, unit):
        base = 0 if unit is None else ra + unit * rb

        def read(at):
            return rz[d, o, pl.ds(pl.multiple_of(base + at.start, 16), 16), :]

        return read

    def rxa_parts(o):
        return [lambda at, k=k: rxa[k - 1, o, at, :] for k in range(1, xs)]

    def step(t, carry):
        for d in (0, 1):
            s = z - t if d == 1 else z + t

            @pl.when((s >= 0) & (s < zs))
            def _():
                for unit in units:
                    gather_z(d, s, unit).wait_recv()

                    @pl.when(has_next(d))
                    def _():
                        gather_z(d, s, unit).start()
                    if unit is None:
                        for k in range(1, xs):
                            gather_xa(k, s, x).start()

        def slab(j, c):
            s = z + t * (1 - 2 * j)

            @pl.when((s >= 0) & (s < zs))
            def _():
                compute(s)
            return c

        lax.fori_loop(0, 2, slab, 0)

        for unit in units:
            def flow(j, c):
                d = jnp.where(z < zs // 2, 1 - j, j)
                o = jnp.where(d == 0, zs - 1 - t, t)
                dist = jnp.where(d == 0, z - o, o - z)
                fed = jnp.where(d == 0, zs - 1 - z, z)

                @pl.when(dist > 0)
                def _():
                    parts = []
                    if unit is None:
                        for k in range(1, xs):
                            reduce_xa(k, o).wait_recv()
                        parts = rxa_parts(o)

                    @pl.when(fed > 0)
                    def _():
                        reduce_z(d, o, unit).wait_recv()
                    read, write = p_part(o, unit)
                    add_rows(ra if unit is None else rb, write, [read, rz_part(d, o, unit)] + parts)
                    reduce_z(d, o, unit).start()
                return c

            lax.fori_loop(0, 2, flow, 0)
        return carry

    lax.fori_loop(1, zs, step, 0)

    def take(unit):
        for d in (0, 1):
            @pl.when(has_next(1 - d))
            def _():
                reduce_z(d, z, unit).wait_recv()

    for k in range(1, xs):
        take(other(k))
        read, write = p_part(z, other(k))
        add_rows(rb, write, [read, rz_part(0, z, other(k)), rz_part(1, z, other(k))])
        reduce_xb(k).start()

    def out_at(base):
        def write(i, value):
            out_ref[pl.ds(pl.multiple_of(base + i, 16), 16), :] = value.astype(out_ref.dtype)
        return write

    take(None)
    for k in range(1, xs):
        reduce_xa(k, z).wait_recv()
    add_rows(
        ra, out_at(0),
        [p_part(z, None)[0], rz_part(0, z, None), rz_part(1, z, None)] + rxa_parts(z),
    )
    take(x)
    for k in range(1, xs):
        reduce_xb(k).wait_recv()
    add_rows(
        rb, out_at(ra),
        [p_part(z, x)[0], rz_part(0, z, x), rz_part(1, z, x)]
        + [lambda at, k=k: rxb[k - 1, at, :] for k in range(1, xs)],
    )

    for k in range(1, xs):
        gather_xb(k, x).wait_send()
        reduce_xb(k).wait_send()

    def sent(s, carry):
        for k in range(1, xs):
            gather_xa(k, s, x).wait_send()
            reduce_xa(k, s).wait_send()
        for d in (0, 1):
            behind = s <= z if d == 1 else s >= z
            ahead = s > z if d == 1 else s < z

            @pl.when(has_next(d) & behind)
            def _():
                for unit in units:
                    gather_z(d, s, unit).wait_send()

            @pl.when(ahead)
            def _():
                for unit in units:
                    reduce_z(d, s, unit).wait_send()
        return carry

    lax.fori_loop(0, zs, sent, 0)


def expert_sum(slot_rows, gate_weight, up_weight, down_weight, tensor):
    rows, width = slot_rows.shape
    hidden = gate_weight.shape[1]
    zs = ROWS_Z if tensor % ROWS_Z == 0 else 1
    xs = tensor // zs
    ra = rows * 5 // 8 // 16 * 16
    rb = rows - ra
    wide = 512 if width % 512 == 0 else 128
    dt = slot_rows.dtype
    dma = pltpu.SemaphoreType.DMA
    flops = 6 * rows * tensor * width * hidden
    return pl.pallas_call(
        functools.partial(expert_kernel, zs, xs, ra, wide),
        out_shape=jax.ShapeDtypeStruct((rows, width), dt),
        in_specs=[pl.BlockSpec(memory_space=pltpu.VMEM)]
        + [pl.BlockSpec(memory_space=pl.ANY)] * 3,
        out_specs=pl.BlockSpec(memory_space=pltpu.VMEM),
        scratch_shapes=[
            pltpu.VMEM((zs, xs * rows, width), dt),
            pltpu.VMEM((zs, xs * rows, width), dt),
            pltpu.VMEM((2, zs, ra + xs * rb, width), dt),
            pltpu.VMEM((xs - 1, zs, ra, width), dt),
            pltpu.VMEM((xs - 1, rb, width), dt),
            pltpu.VMEM((xs * rows, hidden), dt),
            pltpu.VMEM(gate_weight.shape, dt),
            pltpu.VMEM(up_weight.shape, dt),
            pltpu.VMEM(down_weight.shape, dt),
            dma((3,)),
            dma((2, zs, xs + 1)), dma((zs, xs + 1)),
            dma((zs, xs - 1)), dma((zs, xs - 1)),
            dma((xs - 1,)), dma((xs - 1,)),
            dma((2, zs, xs + 1)), dma((2, zs, xs + 1)),
            dma((zs, xs - 1)), dma((zs, xs - 1)),
            dma((xs - 1,)), dma((xs - 1,)),
        ],
        compiler_params=pltpu.CompilerParams(
            collective_id=0, has_side_effects=True, vmem_limit_bytes=60 * 2**20
        ),
        cost_estimate=pl.CostEstimate(
            flops=flops, bytes_accessed=6 * width * hidden + 4 * rows * width,
            transcendentals=rows * tensor * hidden,
        ),
    )(slot_rows, gate_weight, up_weight, down_weight)


def on_device(tensor, tokens, expert_ids, gate_probs, gate_weight, up_weight, down_weight):
    count, width = tokens.shape
    spans = count // CT
    is_window = expert_ids == 0
    routed = jnp.any(is_window, axis=1)
    gate_share = jnp.sum(jnp.where(is_window, gate_probs, 0.0), axis=1)
    routed_blocks = routed.reshape(spans, CT)
    slot_place = jnp.cumsum(routed_blocks.astype(jnp.int32), axis=1) - 1
    selector = (
        (slot_place[:, None, :] == jnp.arange(CAP, dtype=jnp.int32)[None, :, None])
        & routed_blocks[:, None, :]
    ).astype(jnp.bfloat16)
    slot_rows = jnp.einsum(
        "bst,btd->bsd", selector, tokens.reshape(spans, CT, width),
        preferred_element_type=jnp.float32,
    ).astype(jnp.bfloat16)
    expert_out = expert_sum(
        slot_rows.reshape(spans * CAP, width), gate_weight, up_weight, down_weight, tensor
    )
    picked = jnp.einsum(
        "bst,bsd->btd", selector, expert_out.reshape(spans, CAP, width),
        preferred_element_type=jnp.float32,
    )
    mixed = gate_share.reshape(spans, CT)[:, :, None] * picked
    return mixed.astype(jnp.bfloat16).reshape(count, width)


def solution(mesh):
    in_specs = (
        P(("dp", "tensor"), None),
        P(("dp", "tensor"), None),
        P(("dp", "tensor"), None),
        P(None, "tensor"),
        P(None, "tensor"),
        P("tensor", None),
    )
    out_specs = P(("dp", "tensor"), None)
    return jax.shard_map(
        functools.partial(on_device, mesh.shape["tensor"]),
        mesh=mesh, in_specs=in_specs, out_specs=out_specs, check_vma=False,
    )
```

time: 277 us -> 186 us (0.67)
  waiting for transfers between devices: 218 us -> 0 us
  Pallas kernels: 0 us -> 165 us
  matrix products: 27.7 us -> 5.25 us
  between operations: 13.4 us -> 0.02 us
  other arithmetic: 8.61 us -> 1.07 us
  local copies, waits for them, and re-layouts: 9.41 us -> 14.9 us
    pallas_call x0 -> x1, Pallas kernels: none -> 165 us  [expert_sum(): pl.pallas_call(functools.partial(expert_kernel, zs, xs, ra, wide), out_sh...]
    reduce_scatter x1 -> x0, waiting for transfers between devices: 116 us -> none  [on_device(): lax.psum_scatter(partial_rows.astype(jnp.bfloat16), 'tensor', scatter_dim...]
    all_gather x1 -> x0, waiting for transfers between devices: 102 us -> none  [on_device(): lax.all_gather(slot_rows.reshape(SPANS * CAP, model_width), 'tensor', axi...]
    dot_general x3 -> x2, matrix products: 27.7 us -> 5.25 us  [the longest x1 3.83 us: on_device(): jnp.einsum('bst,bsd->btd', selector, expert_out.reshape(spans, CAP, width...]
    unnamed x2 -> x4, local copies, waits for them, and re-layouts: 0.69 us -> 14.9 us
    gather x1 -> x0, local copies, waits for them, and re-layouts: 8.72 us -> none  [on_device(): picked = jnp.take(expert_out, slot_index.reshape(-1), axis=0)]
    convert_element_type x2 -> x0, other arithmetic: 7.3 us -> none  [the longest x1 4.87 us: on_device(): return mixed.astype(jnp.bfloat16)]
  transfers between devices with their start and end apart: 2 -> 0, of which waited for: 2 -> 0; matrix products, arithmetic and copies ran while one was open for 0% -> 0% of each run, Pallas kernels for 0% -> 0%
where the time goes in v1:
time: 186 us
  Pallas kernels  165 us (89%)
  local copies, waits for them, and re-layouts  14.9 us (8%)
  matrix products  5.25 us (3%)
    pallas_call x1, Pallas kernels, expert_sum(): pl.pallas_call(functools.partial(expert_kernel, zs, xs, ra, wide), out_sh...  165 us
    unnamed x4, local copies, waits for them, and re-layouts  14.9 us
    dot_general x1, matrix products, on_device(): jnp.einsum('bst,bsd->btd', selector, expert_out.reshape(spans, CAP, width...  3.83 us

profile of v1, /device:TPU:0, one launch (start us, length us, event | category | flops | bytes accessed | tf_op | source)
XLA Modules:
  0.0 185.9 jit_solution(9426066387479095605)
XLA Ops:
  0.0 0.0 copy-start
  0.0 1.9 %copy-done = bf16[512,3072]{1,0:T(8,128)(2,1)S(1)} copy-done((bf16[512,3072]{1,0:T(8,128)(2,1)S(1)}, bf16[512,3072]{1,0:T(8,128)(2,1)}, u32[]{:S(2)}) %copy-start) | copy-done | bytes 3145752
  1.9 0.7 select_reduce_fusion
  2.7 0.3 reduce_window_sum.11
  3.0 1.4 convolution_convert_fusion
  4.4 6.4 %copy.7.gw_hbm = bf16[3072,672]{1,0:T(8,128)(2,1)} copy(bf16[3072,672]{0,1:T(8,128)(2,1)} %param.9) | data formatting | bytes 8257536 | tf_op args[3]
  10.8 6.5 %copy.8.uw_hbm = bf16[3072,672]{1,0:T(8,128)(2,1)} copy(bf16[3072,672]{0,1:T(8,128)(2,1)} %param.10) | data formatting | bytes 8257536 | tf_op args[4]
  17.4 164.7 %shard_map.64 = bf16[128,3072]{1,0:T(8,128)(2,1)} custom-call(bf16[128,3072]{1,0:T(8,128)(2,1)} %bitcast.11, bf16[3072,672]{1,0:T(8,128)(2,1)} %copy.7.gw_hbm, bf16[3072,672]{1,0:T(8,128)(2,1)} %copy.8.uw_hbm, bf16[672,3072]{1,0:T(8,128)(2,1)} %dw_hbm.1), custom_call_target="tpu_custom_call" | custom-call | flops 12683575296 | bytes 13959168 | tf_op jit(solution)/shard_map/pallas_call | solution.py:326
  182.1 3.8 %multiply_convert_fusion = bf16[4,128,3072]{2,1,0:T(8,128)(2,1)} fusion(bf16[4,32,3072]{2,1,0:T(8,128)(2,1)} %bitcast.10, f32[4,128]{1,0:T(4,128)S(1)} %bitcast.12, s32[4,128]{1,0:T(4,128)S(1)} %broadcast_add_fusion, pred[4,128]{1,0:T(4,128)(4,1)S(1)} %bitcast.14), kind=kOutput, calls=%fused_computation | convolution fusion | flops 103841792 | bytes 3936768 | tf_op jit(solution)/shard_map/bst,bsd->btd/dot_general | solution.py:379
  (3 shorter events, 0.0 us)
Async XLA Ops:
  0.0 1.9 %copy-start = (bf16[512,3072]{1,0:T(8,128)(2,1)S(1)}, bf16[512,3072]{1,0:T(8,128)(2,1)}, u32[]{:S(2)}) copy-start(bf16[512,3072]{1,0:T(8,128)(2,1)} %param.6) | copy-start | bytes 9437188

commit v2 on v1

--- a/solution.py
+++ b/solution.py
@@ -10,7 +10,18 @@
 CT = 128
 CAP = 32
 ROWS_Z = 4
+PIECE = 32
 MESH = pl.DeviceIdType.MESH
+
+
+def cuts(rows):
+    return [(at, min(PIECE, rows - at)) for at in range(0, rows, PIECE)]
+
+
+def dot_t(a, b):
+    return lax.dot_general(
+        a, b, (((1,), (1,)), ((), ())), preferred_element_type=jnp.float32
+    )
 
 
 def expert_kernel(
@@ -22,7 +33,7 @@
 ):
     rows, width = slot_ref.shape
     rb = rows - ra
-    hidden = gw.shape[1]
+    hidden = gw.shape[0]
     me = lax.axis_index("tensor")
     dp = lax.axis_index("dp")
     z = me // xs
@@ -49,10 +60,25 @@
     def unit_sem(unit):
         return 0 if unit is None else 1 + unit
 
-    def slot_rows(unit):
-        if unit is None:
-            return pl.ds(0, ra)
-        return pl.ds(pl.multiple_of(ra + unit * rb, 16), rb)
+    a_cuts = cuts(ra)
+    b_cuts = cuts(rb)
+
+    def a_pieces():
+        return [(None, at, n, i) for i, (at, n) in enumerate(a_cuts)]
+
+    def b_pieces(sx):
+        return [
+            (sx, at, n, len(a_cuts) + sx * len(b_cuts) + i)
+            for i, (at, n) in enumerate(b_cuts)
+        ]
+
+    def p_base(piece):
+        sx, at = piece[:2]
+        return x * rows + at if sx is None else sx * rows + ra + at
+
+    def rz_base(piece):
+        sx, at = piece[:2]
+        return at if sx is None else ra + sx * rb + at
 
     units = [None] + list(range(xs))
 
@@ -87,10 +113,11 @@
             rxb_s.at[k - 1], rxb_r.at[k - 1], dev(z, other(k)),
         )
 
-    def reduce_z(d, o, unit):
-        i = unit_sem(unit)
+    def reduce_z(d, o, piece):
+        n, i = piece[2:]
         return copy(
-            p.at[o, unit_rows(unit)], rz.at[d, o, slot_rows(unit)],
+            p.at[o, pl.ds(pl.multiple_of(p_base(piece), 16), n)],
+            rz.at[d, o, pl.ds(pl.multiple_of(rz_base(piece), 16), n)],
             rz_s.at[d, o, i], rz_r.at[d, o, i], dev(z + 2 * d - 1, x),
         )
 
@@ -146,8 +173,8 @@
         for c in range(0, hidden, 256):
             n = min(256, hidden - c)
             lhs = g[s]
-            gate = jnp.dot(lhs, gw[:, c:c + n], preferred_element_type=jnp.float32)
-            up = jnp.dot(lhs, uw[:, c:c + n], preferred_element_type=jnp.float32)
+            gate = dot_t(lhs, gw[c:c + n, :])
+            up = dot_t(lhs, uw[c:c + n, :])
             h[:, c:c + n] = (gate / (1.0 + jnp.exp(-gate)) * up).astype(h.dtype)
 
         def columns(i, carry):
@@ -177,8 +204,8 @@
 
         lax.fori_loop(0, count // 16, body, 0)
 
-    def p_part(o, unit):
-        base = x * rows if unit is None else unit * rows + ra
+    def p_part(o, piece):
+        base = p_base(piece)
 
         def read(at):
             return p[o, pl.ds(pl.multiple_of(base + at.start, 16), 16), :]
@@ -188,16 +215,22 @@
 
         return read, write
 
-    def rz_part(d, o, unit):
-        base = 0 if unit is None else ra + unit * rb
+    def rz_part(d, o, piece):
+        base = rz_base(piece)
 
         def read(at):
             return rz[d, o, pl.ds(pl.multiple_of(base + at.start, 16), 16), :]
 
         return read
 
-    def rxa_parts(o):
-        return [lambda at, k=k: rxa[k - 1, o, at, :] for k in range(1, xs)]
+    def from_x(ref, first):
+        return lambda at: ref[pl.ds(pl.multiple_of(first + at.start, 16), 16), :]
+
+    def rxa_parts(o, first):
+        return [from_x(rxa.at[k - 1, o], first) for k in range(1, xs)]
+
+    def rxb_parts(first):
+        return [from_x(rxb.at[k - 1], first) for k in range(1, xs)]
 
     def step(t, carry):
         for d in (0, 1):
@@ -225,7 +258,7 @@
 
         lax.fori_loop(0, 2, slab, 0)
 
-        for unit in units:
+        for piece in [q for sx in range(xs) for q in b_pieces(sx)] + a_pieces():
             def flow(j, c):
                 d = jnp.where(z < zs // 2, 1 - j, j)
                 o = jnp.where(d == 0, zs - 1 - t, t)
@@ -235,17 +268,18 @@
                 @pl.when(dist > 0)
                 def _():
                     parts = []
-                    if unit is None:
-                        for k in range(1, xs):
-                            reduce_xa(k, o).wait_recv()
-                        parts = rxa_parts(o)
+                    if piece[0] is None:
+                        if piece[1] == 0:
+                            for k in range(1, xs):
+                                reduce_xa(k, o).wait_recv()
+                        parts = rxa_parts(o, piece[1])
 
                     @pl.when(fed > 0)
                     def _():
-                        reduce_z(d, o, unit).wait_recv()
-                    read, write = p_part(o, unit)
-                    add_rows(ra if unit is None else rb, write, [read, rz_part(d, o, unit)] + parts)
-                    reduce_z(d, o, unit).start()
+                        reduce_z(d, o, piece).wait_recv()
+                    read, write = p_part(o, piece)
+                    add_rows(piece[2], write, [read, rz_part(d, o, piece)] + parts)
+                    reduce_z(d, o, piece).start()
                 return c
 
             lax.fori_loop(0, 2, flow, 0)
@@ -253,16 +287,17 @@
 
     lax.fori_loop(1, zs, step, 0)
 
-    def take(unit):
+    def take(piece):
         for d in (0, 1):
             @pl.when(has_next(1 - d))
             def _():
-                reduce_z(d, z, unit).wait_recv()
-
-    for k in range(1, xs):
-        take(other(k))
-        read, write = p_part(z, other(k))
-        add_rows(rb, write, [read, rz_part(0, z, other(k)), rz_part(1, z, other(k))])
+                reduce_z(d, z, piece).wait_recv()
+
+    for k in range(1, xs):
+        for piece in b_pieces(other(k)):
+            take(piece)
+            read, write = p_part(z, piece)
+            add_rows(piece[2], write, [read, rz_part(0, z, piece), rz_part(1, z, piece)])
         reduce_xb(k).start()
 
     def out_at(base):
@@ -270,21 +305,24 @@
             out_ref[pl.ds(pl.multiple_of(base + i, 16), 16), :] = value.astype(out_ref.dtype)
         return write
 
-    take(None)
     for k in range(1, xs):
         reduce_xa(k, z).wait_recv()
-    add_rows(
-        ra, out_at(0),
-        [p_part(z, None)[0], rz_part(0, z, None), rz_part(1, z, None)] + rxa_parts(z),
-    )
-    take(x)
+    for piece in a_pieces():
+        take(piece)
+        add_rows(
+            piece[2], out_at(piece[1]),
+            [p_part(z, piece)[0], rz_part(0, z, piece), rz_part(1, z, piece)]
+            + rxa_parts(z, piece[1]),
+        )
     for k in range(1, xs):
         reduce_xb(k).wait_recv()
-    add_rows(
-        rb, out_at(ra),
-        [p_part(z, x)[0], rz_part(0, z, x), rz_part(1, z, x)]
-        + [lambda at, k=k: rxb[k - 1, at, :] for k in range(1, xs)],
-    )
+    for piece in b_pieces(x):
+        take(piece)
+        add_rows(
+            piece[2], out_at(ra + piece[1]),
+            [p_part(z, piece)[0], rz_part(0, z, piece), rz_part(1, z, piece)]
+            + rxb_parts(piece[1]),
+        )
 
     for k in range(1, xs):
         gather_xb(k, x).wait_send()
@@ -305,8 +343,8 @@
 
             @pl.when(ahead)
             def _():
-                for unit in units:
-                    reduce_z(d, s, unit).wait_send()
+                for piece in a_pieces() + [q for sx in range(xs) for q in b_pieces(sx)]:
+                    reduce_z(d, s, piece).wait_send()
         return carry
 
     lax.fori_loop(0, zs, sent, 0)
@@ -314,7 +352,7 @@
 
 def expert_sum(slot_rows, gate_weight, up_weight, down_weight, tensor):
     rows, width = slot_rows.shape
-    hidden = gate_weight.shape[1]
+    hidden = gate_weight.shape[0]
     zs = ROWS_Z if tensor % ROWS_Z == 0 else 1
     xs = tensor // zs
     ra = rows * 5 // 8 // 16 * 16
@@ -322,6 +360,7 @@
     wide = 512 if width % 512 == 0 else 128
     dt = slot_rows.dtype
     dma = pltpu.SemaphoreType.DMA
+    pieces = len(cuts(ra)) + xs * len(cuts(rb))
     flops = 6 * rows * tensor * width * hidden
     return pl.pallas_call(
         functools.partial(expert_kernel, zs, xs, ra, wide),
@@ -343,7 +382,7 @@
             dma((2, zs, xs + 1)), dma((zs, xs + 1)),
             dma((zs, xs - 1)), dma((zs, xs - 1)),
             dma((xs - 1,)), dma((xs - 1,)),
-            dma((2, zs, xs + 1)), dma((2, zs, xs + 1)),
+            dma((2, zs, pieces)), dma((2, zs, pieces)),
             dma((zs, xs - 1)), dma((zs, xs - 1)),
             dma((xs - 1,)), dma((xs - 1,)),
         ],
@@ -374,7 +413,7 @@
         preferred_element_type=jnp.float32,
     ).astype(jnp.bfloat16)
     expert_out = expert_sum(
-        slot_rows.reshape(spans * CAP, width), gate_weight, up_weight, down_weight, tensor
+        slot_rows.reshape(spans * CAP, width), gate_weight.T, up_weight.T, down_weight, tensor
     )
     picked = jnp.einsum(
         "bst,bsd->btd", selector, expert_out.reshape(spans, CAP, width),

time: 186 us -> 170 us (0.914)
  local copies, waits for them, and re-layouts: 14.9 us -> 1.89 us
  Pallas kernels: 165 us -> 161 us
    unnamed x4 -> x2, local copies, waits for them, and re-layouts: 14.9 us -> 1.89 us
    pallas_call x1, Pallas kernels: 165 us -> 161 us  [expert_sum(): pl.pallas_call(functools.partial(expert_kernel, zs, xs, ra, wide), out_sh...]
where the time goes in v2:
time: 170 us; the launch traced here: 169 us
  Pallas kernels  161 us (95%)
  matrix products  5.25 us (3%)
  local copies, waits for them, and re-layouts  1.89 us (1%)
    pallas_call x1, Pallas kernels, expert_sum(): pl.pallas_call(functools.partial(expert_kernel, zs, xs, ra, wide), out_sh...  161 us
    dot_general x1, matrix products, on_device(): jnp.einsum('bst,bsd->btd', selector, expert_out.reshape(spans, CAP, width...  3.83 us

profile of v2, /device:TPU:0, one launch (start us, length us, event | category | flops | bytes accessed | tf_op | source)
XLA Modules:
  0.0 169.1 jit_solution(9050690293067208058)
XLA Ops:
  0.0 0.0 copy-start
  0.0 1.9 %copy-done = bf16[512,3072]{1,0:T(8,128)(2,1)S(1)} copy-done((bf16[512,3072]{1,0:T(8,128)(2,1)S(1)}, bf16[512,3072]{1,0:T(8,128)(2,1)}, u32[]{:S(2)}) %copy-start) | copy-done | bytes 3145752
  1.9 0.7 select_reduce_fusion
  2.7 0.3 reduce_window_sum.11
  3.0 1.4 convolution_convert_fusion
  4.4 160.9 %shard_map.64 = bf16[128,3072]{1,0:T(8,128)(2,1)} custom-call(bf16[128,3072]{1,0:T(8,128)(2,1)} %bitcast.13, bf16[672,3072]{1,0:T(8,128)(2,1)} %bitcast.17, bf16[672,3072]{1,0:T(8,128)(2,1)} %bitcast.18, bf16[672,3072]{1,0:T(8,128)(2,1)} %dw_hbm.1), custom_call_target="tpu_custom_call" | custom-call | flops 12683575296 | bytes 13959168 | tf_op jit(solution)/shard_map/pallas_call | solution.py:365
  165.3 3.8 %multiply_convert_fusion = bf16[4,128,3072]{2,1,0:T(8,128)(2,1)} fusion(bf16[4,32,3072]{2,1,0:T(8,128)(2,1)} %bitcast.12, f32[4,128]{1,0:T(4,128)S(1)} %bitcast.14, s32[4,128]{1,0:T(4,128)S(1)} %broadcast_add_fusion, pred[4,128]{1,0:T(4,128)(4,1)S(1)} %bitcast.16), kind=kOutput, calls=%fused_computation | convolution fusion | flops 103841792 | bytes 3936768 | tf_op jit(solution)/shard_map/bst,bsd->btd/dot_general | solution.py:418
  (3 shorter events, 0.0 us)
Async XLA Ops:
  0.0 1.9 %copy-start = (bf16[512,3072]{1,0:T(8,128)(2,1)S(1)}, bf16[512,3072]{1,0:T(8,128)(2,1)}, u32[]{:S(2)}) copy-start(bf16[512,3072]{1,0:T(8,128)(2,1)} %param.6) | copy-start | bytes 9437188

commit v3 on v2

--- a/solution.py
+++ b/solution.py
@@ -233,12 +233,12 @@
         return [from_x(rxb.at[k - 1], first) for k in range(1, xs)]
 
     def step(t, carry):
-        for d in (0, 1):
-            s = z - t if d == 1 else z + t
-
-            @pl.when((s >= 0) & (s < zs))
-            def _():
-                for unit in units:
+        for unit in units:
+            for d in (0, 1):
+                s = z - t if d == 1 else z + t
+
+                @pl.when((s >= 0) & (s < zs))
+                def _():
                     gather_z(d, s, unit).wait_recv()
 
                     @pl.when(has_next(d))
@@ -249,9 +249,10 @@
                             gather_xa(k, s, x).start()
 
         def slab(j, c):
-            s = z + t * (1 - 2 * j)
-
-            @pl.when((s >= 0) & (s < zs))
+            far = jnp.where(z < zs // 2, 1, -1)
+            s = jnp.where(j == 0, z - far * (t - 1), z + far * t)
+
+            @pl.when((s >= 0) & (s < zs) & (j + t >= 2))
             def _():
                 compute(s)
             return c

time: 170 us -> 164 us (0.965)
  Pallas kernels: 161 us -> 154 us
    pallas_call x1, Pallas kernels: 161 us -> 154 us  [expert_sum(): pl.pallas_call(functools.partial(expert_kernel, zs, xs, ra, wide), out_sh...]
where the time goes in v3:
time: 164 us; the launch traced here: 162 us
  Pallas kernels  154 us (94%)
  matrix products  5.25 us (3%)
  local copies, waits for them, and re-layouts  1.89 us (1%)
    pallas_call x1, Pallas kernels, expert_sum(): pl.pallas_call(functools.partial(expert_kernel, zs, xs, ra, wide), out_sh...  154 us
    dot_general x1, matrix products, on_device(): jnp.einsum('bst,bsd->btd', selector, expert_out.reshape(spans, CAP, width...  3.83 us

profile of v3, /device:TPU:0, one launch (start us, length us, event | category | flops | bytes accessed | tf_op | source)
XLA Modules:
  0.0 161.8 jit_solution(12919400272955691730)
XLA Ops:
  0.0 0.0 copy-start
  0.0 1.9 %copy-done = bf16[512,3072]{1,0:T(8,128)(2,1)S(1)} copy-done((bf16[512,3072]{1,0:T(8,128)(2,1)S(1)}, bf16[512,3072]{1,0:T(8,128)(2,1)}, u32[]{:S(2)}) %copy-start) | copy-done | bytes 3145752
  1.9 0.7 select_reduce_fusion
  2.7 0.3 reduce_window_sum.11
  3.0 1.4 convolution_convert_fusion
  4.4 153.6 %shard_map.64 = bf16[128,3072]{1,0:T(8,128)(2,1)} custom-call(bf16[128,3072]{1,0:T(8,128)(2,1)} %bitcast.13, bf16[672,3072]{1,0:T(8,128)(2,1)} %bitcast.17, bf16[672,3072]{1,0:T(8,128)(2,1)} %bitcast.18, bf16[672,3072]{1,0:T(8,128)(2,1)} %dw_hbm.1), custom_call_target="tpu_custom_call" | custom-call | flops 12683575296 | bytes 13959168 | tf_op jit(solution)/shard_map/pallas_call | solution.py:366
  158.0 3.8 %multiply_convert_fusion = bf16[4,128,3072]{2,1,0:T(8,128)(2,1)} fusion(bf16[4,32,3072]{2,1,0:T(8,128)(2,1)} %bitcast.12, f32[4,128]{1,0:T(4,128)S(1)} %bitcast.14, s32[4,128]{1,0:T(4,128)S(1)} %broadcast_add_fusion, pred[4,128]{1,0:T(4,128)(4,1)S(1)} %bitcast.16), kind=kOutput, calls=%fused_computation | convolution fusion | flops 103841792 | bytes 3936768 | tf_op jit(solution)/shard_map/bst,bsd->btd/dot_general | solution.py:419
  (3 shorter events, 0.0 us)
Async XLA Ops:
  0.0 1.9 %copy-start = (bf16[512,3072]{1,0:T(8,128)(2,1)S(1)}, bf16[512,3072]{1,0:T(8,128)(2,1)}, u32[]{:S(2)}) copy-start(bf16[512,3072]{1,0:T(8,128)(2,1)} %param.6) | copy-start | bytes 9437188

commit v4 on v3

--- a/solution.py
+++ b/solution.py
@@ -10,7 +10,7 @@
 CT = 128
 CAP = 32
 ROWS_Z = 4
-PIECE = 32
+PIECE = 16
 MESH = pl.DeviceIdType.MESH
 
 

time: 164 us -> 175 us (1.067); the launches traced: 162 us -> 175 us
  Pallas kernels: 154 us -> 167 us
    pallas_call x1, Pallas kernels: 154 us -> 167 us  [expert_sum(): pl.pallas_call(functools.partial(expert_kernel, zs, xs, ra, wide), out_sh...]
where the time goes in v4:
time: 175 us
  Pallas kernels  167 us (95%)
  matrix products  5.25 us (3%)
  local copies, waits for them, and re-layouts  1.89 us (1%)
    pallas_call x1, Pallas kernels, expert_sum(): pl.pallas_call(functools.partial(expert_kernel, zs, xs, ra, wide), out_sh...  167 us
    dot_general x1, matrix products, on_device(): jnp.einsum('bst,bsd->btd', selector, expert_out.reshape(spans, CAP, width...  3.83 us

profile of v4, /device:TPU:0, one launch (start us, length us, event | category | flops | bytes accessed | tf_op | source)
XLA Modules:
  0.0 174.7 jit_solution(11168775009631586167)
XLA Ops:
  0.0 0.0 copy-start
  0.0 1.9 %copy-done = bf16[512,3072]{1,0:T(8,128)(2,1)S(1)} copy-done((bf16[512,3072]{1,0:T(8,128)(2,1)S(1)}, bf16[512,3072]{1,0:T(8,128)(2,1)}, u32[]{:S(2)}) %copy-start) | copy-done | bytes 3145752
  1.9 0.7 select_reduce_fusion
  2.7 0.3 reduce_window_sum.11
  3.0 1.4 convolution_convert_fusion
  4.4 166.5 %shard_map.64 = bf16[128,3072]{1,0:T(8,128)(2,1)} custom-call(bf16[128,3072]{1,0:T(8,128)(2,1)} %bitcast.13, bf16[672,3072]{1,0:T(8,128)(2,1)} %bitcast.17, bf16[672,3072]{1,0:T(8,128)(2,1)} %bitcast.18, bf16[672,3072]{1,0:T(8,128)(2,1)} %dw_hbm.1), custom_call_target="tpu_custom_call" | custom-call | flops 12683575296 | bytes 13959168 | tf_op jit(solution)/shard_map/pallas_call | solution.py:366
  170.9 3.8 %multiply_convert_fusion = bf16[4,128,3072]{2,1,0:T(8,128)(2,1)} fusion(bf16[4,32,3072]{2,1,0:T(8,128)(2,1)} %bitcast.12, f32[4,128]{1,0:T(4,128)S(1)} %bitcast.14, s32[4,128]{1,0:T(4,128)S(1)} %broadcast_add_fusion, pred[4,128]{1,0:T(4,128)(4,1)S(1)} %bitcast.16), kind=kOutput, calls=%fused_computation | convolution fusion | flops 103841792 | bytes 3936768 | tf_op jit(solution)/shard_map/bst,bsd->btd/dot_general | solution.py:419
  (3 shorter events, 0.0 us)
Async XLA Ops:
  0.0 1.9 %copy-start = (bf16[512,3072]{1,0:T(8,128)(2,1)S(1)}, bf16[512,3072]{1,0:T(8,128)(2,1)}, u32[]{:S(2)}) copy-start(bf16[512,3072]{1,0:T(8,128)(2,1)} %param.6) | copy-start | bytes 9437188

commit v5 on v4

--- a/solution.py
+++ b/solution.py
@@ -10,7 +10,7 @@
 CT = 128
 CAP = 32
 ROWS_Z = 4
-PIECE = 16
+PIECE = 48
 MESH = pl.DeviceIdType.MESH
 
 

time: 175 us -> 160 us (0.914)
  Pallas kernels: 167 us -> 151 us
    pallas_call x1, Pallas kernels: 167 us -> 151 us  [expert_sum(): pl.pallas_call(functools.partial(expert_kernel, zs, xs, ra, wide), out_sh...]
where the time goes in v5:
time: 160 us; the launch traced here: 159 us
  Pallas kernels  151 us (94%)
  matrix products  5.25 us (3%)
  local copies, waits for them, and re-layouts  1.89 us (1%)
    pallas_call x1, Pallas kernels, expert_sum(): pl.pallas_call(functools.partial(expert_kernel, zs, xs, ra, wide), out_sh...  151 us
    dot_general x1, matrix products, on_device(): jnp.einsum('bst,bsd->btd', selector, expert_out.reshape(spans, CAP, width...  3.83 us

profile of v5, /device:TPU:0, one launch (start us, length us, event | category | flops | bytes accessed | tf_op | source)
XLA Modules:
  0.0 159.2 jit_solution(8414643753570230400)
XLA Ops:
  0.0 0.0 copy-start
  0.0 1.9 %copy-done = bf16[512,3072]{1,0:T(8,128)(2,1)S(1)} copy-done((bf16[512,3072]{1,0:T(8,128)(2,1)S(1)}, bf16[512,3072]{1,0:T(8,128)(2,1)}, u32[]{:S(2)}) %copy-start) | copy-done | bytes 3145752
  1.9 0.7 select_reduce_fusion
  2.7 0.3 reduce_window_sum.11
  3.0 1.4 convolution_convert_fusion
  4.4 151.0 %shard_map.64 = bf16[128,3072]{1,0:T(8,128)(2,1)} custom-call(bf16[128,3072]{1,0:T(8,128)(2,1)} %bitcast.13, bf16[672,3072]{1,0:T(8,128)(2,1)} %bitcast.17, bf16[672,3072]{1,0:T(8,128)(2,1)} %bitcast.18, bf16[672,3072]{1,0:T(8,128)(2,1)} %dw_hbm.1), custom_call_target="tpu_custom_call" | custom-call | flops 12683575296 | bytes 13959168 | tf_op jit(solution)/shard_map/pallas_call | solution.py:366
  155.4 3.8 %multiply_convert_fusion = bf16[4,128,3072]{2,1,0:T(8,128)(2,1)} fusion(bf16[4,32,3072]{2,1,0:T(8,128)(2,1)} %bitcast.12, f32[4,128]{1,0:T(4,128)S(1)} %bitcast.14, s32[4,128]{1,0:T(4,128)S(1)} %broadcast_add_fusion, pred[4,128]{1,0:T(4,128)(4,1)S(1)} %bitcast.16), kind=kOutput, calls=%fused_computation | convolution fusion | flops 103841792 | bytes 3936768 | tf_op jit(solution)/shard_map/bst,bsd->btd/dot_general | solution.py:419
  (3 shorter events, 0.0 us)
Async XLA Ops:
  0.0 1.9 %copy-start = (bf16[512,3072]{1,0:T(8,128)(2,1)S(1)}, bf16[512,3072]{1,0:T(8,128)(2,1)}, u32[]{:S(2)}) copy-start(bf16[512,3072]{1,0:T(8,128)(2,1)} %param.6) | copy-start | bytes 9437188

commit v6 on v5

--- a/solution.py
+++ b/solution.py
@@ -10,7 +10,7 @@
 CT = 128
 CAP = 32
 ROWS_Z = 4
-PIECE = 48
+PIECE = 80
 MESH = pl.DeviceIdType.MESH
 
 

time: 160 us -> 161 us (level)
  no operation moved by 1% of the time
where the time goes in v6:
time: 161 us; the launch traced here: 160 us
  Pallas kernels  152 us (94%)
  matrix products  5.25 us (3%)
  local copies, waits for them, and re-layouts  1.89 us (1%)
    pallas_call x1, Pallas kernels, expert_sum(): pl.pallas_call(functools.partial(expert_kernel, zs, xs, ra, wide), out_sh...  152 us
    dot_general x1, matrix products, on_device(): jnp.einsum('bst,bsd->btd', selector, expert_out.reshape(spans, CAP, width...  3.83 us

profile of v6, /device:TPU:0, one launch (start us, length us, event | category | flops | bytes accessed | tf_op | source)
XLA Modules:
  0.0 160.5 jit_solution(11041084825950067168)
XLA Ops:
  0.0 0.0 copy-start
  0.0 1.9 %copy-done = bf16[512,3072]{1,0:T(8,128)(2,1)S(1)} copy-done((bf16[512,3072]{1,0:T(8,128)(2,1)S(1)}, bf16[512,3072]{1,0:T(8,128)(2,1)}, u32[]{:S(2)}) %copy-start) | copy-done | bytes 3145752
  1.9 0.7 select_reduce_fusion
  2.7 0.3 reduce_window_sum.11
  3.0 1.4 convolution_convert_fusion
  4.4 152.2 %shard_map.64 = bf16[128,3072]{1,0:T(8,128)(2,1)} custom-call(bf16[128,3072]{1,0:T(8,128)(2,1)} %bitcast.13, bf16[672,3072]{1,0:T(8,128)(2,1)} %bitcast.17, bf16[672,3072]{1,0:T(8,128)(2,1)} %bitcast.18, bf16[672,3072]{1,0:T(8,128)(2,1)} %dw_hbm.1), custom_call_target="tpu_custom_call" | custom-call | flops 12683575296 | bytes 13959168 | tf_op jit(solution)/shard_map/pallas_call | solution.py:366
  156.6 3.8 %multiply_convert_fusion = bf16[4,128,3072]{2,1,0:T(8,128)(2,1)} fusion(bf16[4,32,3072]{2,1,0:T(8,128)(2,1)} %bitcast.12, f32[4,128]{1,0:T(4,128)S(1)} %bitcast.14, s32[4,128]{1,0:T(4,128)S(1)} %broadcast_add_fusion, pred[4,128]{1,0:T(4,128)(4,1)S(1)} %bitcast.16), kind=kOutput, calls=%fused_computation | convolution fusion | flops 103841792 | bytes 3936768 | tf_op jit(solution)/shard_map/bst,bsd->btd/dot_general | solution.py:419
  (3 shorter events, 0.0 us)
Async XLA Ops:
  0.0 1.9 %copy-start = (bf16[512,3072]{1,0:T(8,128)(2,1)S(1)}, bf16[512,3072]{1,0:T(8,128)(2,1)}, u32[]{:S(2)}) copy-start(bf16[512,3072]{1,0:T(8,128)(2,1)} %param.6) | copy-start | bytes 9437188
